TPU v7x, 32 devices: a whole 2x2x4 slice. The times are simulated.
32 devices in a mesh: blk: 4 (over z), pen: 8 (over y, x, core).
Axes of the slice: x: 2, y: 2, z: 4, core: 2. Of those that a mesh axis runs over, the one named last changes fastest.
Arguments:
- state: bfloat16 [4, 2, 32, 512, 512], P('blk', None, None, 'pen'), may hold values from -6 to 6
- inverse_x: bfloat16 [4, 2, 512, 512], P('blk')
- inverse_y: bfloat16 [4, 2, 512, 512], P('blk')
- rates: float32 [4, 3], P('blk'), may hold values from 0.05 to 0.4
- partner: int32 [4, 2], P('blk'), may hold values from 0 to 3
- face_side: int32 [4, 2], P('blk'), may hold values from 0 to 1
- orient: int32 [4, 2], P('blk'), may hold values from 0 to 1
- offset: int32 [4, 2], P('blk'), may hold values from 0 to 7
Outputs:
- relaxed: bfloat16 [4, 2, 32, 512, 512], P('blk', None, None, 'pen')
All inputs are finite; a program needn't handle non-finite values.
Results may differ from a plain program's by a relative error of at most 0.0058.
Values may be sent and summed in bfloat16 or wider, within the bound.
A program may use at most 64 MiB of HBM per device.

v0:
```python
import jax
import jax.numpy as jnp
from jax import lax
from jax.sharding import PartitionSpec as P

STEPS = 2


def plane_ghosts(layers, partner_row, side_row, orient_row, offset_row, tile_rows):
    blocks = lax.all_gather(layers[None], "blk", axis=0, tiled=True)
    lines = layers.shape[-1]
    rows_y = jnp.arange(lines, dtype=jnp.int32)
    result = []
    for which in range(2):
        piece = lax.dynamic_index_in_dim(blocks, partner_row[which], 0, keepdims=False)
        segment = lax.dynamic_index_in_dim(piece, side_row[which], 0, keepdims=False)
        mirrored = jnp.where(orient_row[which] == 1, lines - 1 - rows_y, rows_y)
        take_at = (mirrored + offset_row[which] * tile_rows) % lines
        result.append(jnp.take(segment, take_at, axis=-1))
    return result


def local(state, inverse_x, inverse_y, rates, partner, face_side, orient, offset):
    magnet = state[0]
    inv_x = inverse_x[0]
    inv_y = inverse_y[0]
    rate_row = rates[0]
    first_col = inv_x[:, :, 0].astype(jnp.float32)
    last_col = inv_x[:, :, -1].astype(jnp.float32)
    tile_rows = magnet.shape[2]
    planes = lax.all_to_all(magnet, "pen", split_axis=1, concat_axis=2, tiled=True)
    for repeat in range(STEPS):
        layers = jnp.stack([planes[..., 0], planes[..., -1]], axis=0)
        ghosts = plane_ghosts(layers, partner[0], face_side[0], orient[0], offset[0], tile_rows)
        interior = jnp.einsum("fax,fzyx->fzya", inv_x, planes, preferred_element_type=jnp.float32)
        edges = first_col[:, None, None, :] * ghosts[0].astype(jnp.float32)[..., None]
        edges = edges + last_col[:, None, None, :] * ghosts[1].astype(jnp.float32)[..., None]
        swept_x = (interior + edges).astype(jnp.bfloat16)
        swept_y = jnp.einsum("fcy,fzyx->fzcx", inv_y, swept_x, preferred_element_type=jnp.float32)
        proton = swept_y[0]
        carbon = swept_y[1]
        new_proton = proton - (rate_row[0] * proton + rate_row[2] * carbon)
        new_carbon = carbon - (rate_row[1] * carbon + rate_row[2] * proton)
        planes = jnp.stack([new_proton, new_carbon]).astype(jnp.bfloat16)
    magnet = lax.all_to_all(planes, "pen", split_axis=2, concat_axis=1, tiled=True)
    return magnet[None]


def solution(mesh):
    return jax.shard_map(
        local,
        mesh=mesh,
        in_specs=(
            P("blk", None, None, "pen", None),
            P("blk", None, None, None),
            P("blk", None, None, None),
            P("blk", None),
            P("blk", None),
            P("blk", None),
            P("blk", None),
            P("blk", None),
        ),
        out_specs=P("blk", None, None, "pen", None),
        check_vma=False,
    )
```

profile of v0, /device:TPU:1, one launch (start us, length us, event | category | flops | bytes accessed | tf_op | source)
XLA Modules:
  0.0 204.0 jit_solution(9170097054782782602)
XLA Ops:
  0.0 0.0 copy-start
  0.0 4.8 %copy.84 = bf16[1,2,32,64,512]{4,3,1,2,0:T(8,128)(2,1)} copy(bf16[1,2,32,64,512]{4,3,2,1,0:T(8,128)(2,1)} %param.10) | data formatting | bytes 8388608 | tf_op args[0]
  4.8 0.0 copy-start.6
  4.8 0.0 copy-start.7
  4.8 0.0 copy-start.8
  4.8 0.0 copy-start.9
  4.8 0.0 copy-start.5
  4.8 0.0 copy-start.4
  4.8 5.4 %all-to-all-start = ((bf16[2,32,64,512]{3,2,0,1:T(8,128)(2,1)}), bf16[2,32,64,512]{3,2,0,1:T(8,128)(2,1)}, u32[]{:S(2)}, u32[]{:S(2)}) async-start(bf16[2,32,64,512]{3,2,0,1:T(8,128)(2,1)} %bitcast.67), calls=%async_computation | async-start | bytes 8388608 | tf_op jit(solution)/shard_map/all_to_all | solution.py:31
  10.2 0.0 copy-done.6
  10.2 0.6 fusion.38
  13.2 0.0 copy-done.7
  13.2 0.7 fusion.37
  18.9 0.0 copy-done.8
  18.9 0.6 fusion.35
  20.8 0.0 copy-done.9
  20.8 0.6 fusion.36
  22.7 0.0 copy-done.5
  22.8 0.6 fusion.34
  23.4 0.0 copy-done.4
  23.4 0.3 convert_reduce_fusion.1
  23.7 32.2 %all-to-all-done = bf16[2,32,64,512]{3,2,0,1:T(8,128)(2,1)} async-done(((bf16[2,32,64,512]{3,2,0,1:T(8,128)(2,1)}), bf16[2,32,64,512]{3,2,0,1:T(8,128)(2,1)}, u32[]{:S(2)}, u32[]{:S(2)}) %all-to-all-start) | async-done | bytes 4194336 | tf_op jit(solution)/shard_map/all_to_all | solution.py:31
  55.9 2.7 %copy.54 = bf16[2,4,8,64,512]{4,3,2,1,0:T(8,128)(2,1)S(1)} copy(bf16[2,4,8,64,512]{4,3,0,1,2:T(8,128)(2,1)} %bitcast.3) | data formatting | bytes 8388608 | tf_op jit(solution)/shard_map/all_to_all | solution.py:31
  58.5 0.0 copy-start.2
  58.5 2.0 copy-done.2
  60.6 1.1 slice_reduce_fusion.1
  61.6 11.2 %all-gather = bf16[8,2,4,512]{3,2,1,0:T(4,128)(2,1)S(1)} all-gather(bf16[2,2,4,512]{3,2,1,0:T(4,128)(2,1)S(1)} %pad_maximum_fusion.3), channel_id=2, replica_groups=mesh['blk'=4,'pen'=8] {'blk'}, dimensions={0}, use_global_device_ids=true | all-gather | bytes 81920 | tf_op jit(solution)/shard_map/all_gather | solution.py:10
  72.8 0.2 copy.77
  73.1 2.1 %gather_fusion = bf16[512,2,4]{2,1,0:T(2,128)(2,1)S(1)} fusion(bf16[2,4,512]{1,0,2:T(2,128)(2,1)S(1)} %bitcast.73, s32[1024]{0:T(1024)S(1)} %pad_clamp_fusion.1), kind=kCustom, calls=%fused_computation.clone | custom fusion | bytes 18432 | tf_op jit(solution)/shard_map/jit(_take)/gather | solution.py:19
  75.2 0.1 copy.56
  75.3 0.2 copy.78
  75.6 2.1 %gather_fusion.1 = bf16[512,2,4]{2,1,0:T(2,128)(2,1)S(1)} fusion(bf16[2,4,512]{1,0,2:T(2,128)(2,1)S(1)} %bitcast.74, s32[1024]{0:T(1024)S(1)} %pad_clamp_fusion), kind=kCustom, calls=%fused_computation.1.clone | custom fusion | bytes 18432 | tf_op jit(solution)/shard_map/jit(_take)/gather | solution.py:19
  77.7 0.1 copy.58
  77.9 0.0 copy-done
  77.9 9.2 %fusion.18 = f32[2,4,512,512]{2,3,1,0:T(8,128)} fusion(f32[2,4,512]{2,1,0:T(4,128)S(1)} %get-tuple-element.31, f32[2,512]{1,0:T(2,128)S(1)} %get-tuple-element.9, f32[2,4,512]{2,1,0:T(4,128)S(1)} %get-tuple-element.32, f32[2,512]{1,0:T(2,128)S(1)} %get-tuple-element.8, bf16[2,4,512,512]{3,2,1,0:T(8,128)(2,1)} %bitcast.70, ...), kind=kOutput, calls=%fused_computation.26 | convolution fusion | flops 4305453056 | bytes 14721024 | tf_op jit(solution)/shard_map/fcy,fzyx->fzcx/dot_general | solution.py:39
  87.1 6.0 %subtract_convert_fusion.3 = (bf16[1,4,512,512]{2,3,1,0:T(8,128)(2,1)S(1)}, bf16[1,4,512,512]{2,3,1,0:T(8,128)(2,1)S(1)}) fusion(f32[2,4,512,512]{2,3,1,0:T(8,128)} %fusion.18, f32[]{:T(128)} %bitcast.26, f32[]{:T(128)} %bitcast.25, f32[]{:T(128)} %bitcast.27), kind=kLoop, calls=%fused_computation.19 | loop fusion | flops 10485760 | bytes 12582924 | tf_op jit(solution)/shard_map/convert.4
  93.1 0.0 copy-start.3
  93.1 1.3 copy-done.3
  94.5 10.6 %all-gather.1 = bf16[8,2,4,512]{3,2,1,0:T(4,128)(2,1)S(1)} all-gather(bf16[2,2,4,512]{3,2,1,0:T(4,128)(2,1)S(1)} %pad_maximum_fusion.4), channel_id=3, replica_groups=mesh['blk'=4,'pen'=8] {'blk'}, dimensions={0}, use_global_device_ids=true | all-gather | bytes 81920 | tf_op jit(solution)/shard_map/all_gather | solution.py:10
  105.1 0.2 copy.79
  105.3 2.4 %gather_fusion.2 = bf16[512,2,4]{2,1,0:T(2,128)(2,1)} fusion(bf16[2,4,512]{1,0,2:T(2,128)(2,1)S(1)} %bitcast.71, s32[1024]{0:T(1024)S(1)} %pad_clamp_fusion.1), kind=kCustom, calls=%fused_computation.2.clone | custom fusion | bytes 18432 | tf_op jit(solution)/shard_map/jit(_take)/gather | solution.py:19
  107.7 1.1 copy.62
  108.9 0.2 copy.80
  109.1 2.4 %gather_fusion.3 = bf16[512,2,4]{2,1,0:T(2,128)(2,1)} fusion(bf16[2,4,512]{1,0,2:T(2,128)(2,1)S(1)} %bitcast.72, s32[1024]{0:T(1024)S(1)} %pad_clamp_fusion), kind=kCustom, calls=%fused_computation.3.clone | custom fusion | bytes 18432 | tf_op jit(solution)/shard_map/jit(_take)/gather | solution.py:19
  111.5 1.1 copy.64
  112.7 10.5 %fusion.19 = f32[2,4,512,512]{2,3,1,0:T(8,128)} fusion(f32[2,4,512]{2,1,0:T(4,128)S(1)} %bitcast_convert_fusion, f32[2,4,512]{2,1,0:T(4,128)S(1)} %bitcast_convert_fusion.1, f32[2,512]{1,0:T(2,128)S(1)} %get-tuple-element.9, f32[2,512]{1,0:T(2,128)S(1)} %get-tuple-element.8, bf16[1,4,512,512]{2,3,1,0:T(8,128)(2,1)} %copy-done.3, ...), kind=kOutput, calls=%fused_computation.27 | convolution fusion | flops 4307550208 | bytes 14721024 | tf_op jit(solution)/shard_map/fcy,fzyx->fzcx/dot_general | solution.py:39
  123.2 6.0 %subtract_convert_fusion.1 = (bf16[1,4,512,512]{2,3,1,0:T(8,128)(2,1)S(1)}, bf16[1,4,512,512]{2,3,1,0:T(8,128)(2,1)S(1)}) fusion(f32[2,4,512,512]{2,3,1,0:T(8,128)} %fusion.19, f32[]{:T(128)} %bitcast.26, f32[]{:T(128)} %bitcast.25, f32[]{:T(128)} %bitcast.27), kind=kLoop, calls=%fused_computation.15 | loop fusion | flops 10485760 | bytes 12582924 | tf_op jit(solution)/shard_map/convert.2
  129.1 2.4 %pad_maximum_fusion = bf16[2,4,512,512]{2,3,1,0:T(8,128)(2,1)} fusion(bf16[1,4,512,512]{2,3,1,0:T(8,128)(2,1)S(1)} %get-tuple-element.11, bf16[1,4,512,512]{2,3,1,0:T(8,128)(2,1)S(1)} %get-tuple-element.10), kind=kLoop, calls=%fused_computation.12 | loop fusion | flops 2097152 | bytes 8388608 | tf_op jit(solution)/shard_map/stack | solution.py:44
  131.5 7.9 %copy.66 = bf16[2,4,512,512]{3,1,0,2:T(4,128)(2,1)} copy(bf16[2,4,512,512]{2,3,1,0:T(8,128)(2,1)} %pad_maximum_fusion) | data formatting | bytes 8388608 | tf_op jit(solution)/shard_map/stack | solution.py:44
  139.4 60.7 %all_to_all.33 = bf16[2,4,512,512]{3,1,0,2:T(4,128)(2,1)S(1)} all-to-all(bf16[2,4,512,512]{3,1,0,2:T(4,128)(2,1)} %copy.66), channel_id=1, replica_groups=mesh['blk'=4,'pen'=8] {'pen'}, dimensions={2} | all-to-all | bytes 8388608 | tf_op jit(solution)/shard_map/all_to_all | solution.py:45
  200.1 1.4 copy.67
  201.5 0.0 copy-start.1
  201.5 2.5 %copy.68 = bf16[2,8,4,64,512]{4,3,2,1,0:T(8,128)(2,1)} copy(bf16[2,8,4,64,512]{4,3,1,2,0:T(8,128)(2,1)S(1)} %bitcast.68) | data formatting | bytes 8388608 | tf_op jit(solution)/shard_map/all_to_all | solution.py:45
  204.0 0.0 copy-done.1
  (16 shorter events, 0.3 us)
Async XLA Ops:
  0.0 77.9 %copy-start = (bf16[1,2,512,512]{3,2,1,0:T(8,128)(2,1)S(1)}, bf16[1,2,512,512]{3,2,1,0:T(8,128)(2,1)}, u32[]{:S(2)}) copy-start(bf16[1,2,512,512]{3,2,1,0:T(8,128)(2,1)} %param.12) | copy-start | bytes 3145732
  4.8 5.4 %copy-start.6 = (s32[1,2]{1,0:T(1,128)S(1)}, s32[1,2]{1,0:T(1,128)}, u32[]{:S(2)}) copy-start(s32[1,2]{1,0:T(1,128)} %param.14) | copy-start | bytes 28
  4.8 8.4 %copy-start.7 = (s32[1,2]{1,0:T(1,128)S(1)}, s32[1,2]{1,0:T(1,128)}, u32[]{:S(2)}) copy-start(s32[1,2]{1,0:T(1,128)} %param.15) | copy-start | bytes 28
  4.8 14.1 %copy-start.8 = (s32[1,2]{1,0:T(1,128)S(1)}, s32[1,2]{1,0:T(1,128)}, u32[]{:S(2)}) copy-start(s32[1,2]{1,0:T(1,128)} %param.16) | copy-start | bytes 28
  4.8 16.0 %copy-start.9 = (s32[1,2]{1,0:T(1,128)S(1)}, s32[1,2]{1,0:T(1,128)}, u32[]{:S(2)}) copy-start(s32[1,2]{1,0:T(1,128)} %param.17) | copy-start | bytes 28
  4.8 17.9 %copy-start.5 = (f32[1,3]{1,0:T(1,128)S(1)}, f32[1,3]{1,0:T(1,128)}, u32[]{:S(2)}) copy-start(f32[1,3]{1,0:T(1,128)} %param.13) | copy-start | bytes 40
  4.8 18.5 %copy-start.4 = (bf16[1,2,512,512]{3,2,1,0:T(8,128)(2,1)S(1)}, bf16[1,2,512,512]{3,2,1,0:T(8,128)(2,1)}, u32[]{:S(2)}) copy-start(bf16[1,2,512,512]{3,2,1,0:T(8,128)(2,1)} %param.11) | copy-start | bytes 3145732
  4.8 51.0 %all-to-all-start = ((bf16[2,32,64,512]{3,2,0,1:T(8,128)(2,1)}), bf16[2,32,64,512]{3,2,0,1:T(8,128)(2,1)}, u32[]{:S(2)}, u32[]{:S(2)}) async-start(bf16[2,32,64,512]{3,2,0,1:T(8,128)(2,1)} %bitcast.67), calls=%async_computation | async-start | bytes 8388608 | tf_op jit(solution)/shard_map/all_to_all | solution.py:31
  58.5 2.0 copy-start.2
  93.1 1.3 copy-start.3
  201.5 2.5 %copy-start.1 = (bf16[1,2,512,512]{3,2,1,0:T(8,128)(2,1)S(1)}, bf16[1,2,512,512]{3,2,1,0:T(8,128)(2,1)}, u32[]{:S(2)}) copy-start(bf16[1,2,512,512]{3,2,1,0:T(8,128)(2,1)} %param.12) | copy-start | bytes 3145732
where the time goes:
time: 206 us; the launch traced here: 204 us
  blocking collectives  82.5 us (40%)
  local copies, waits for them, and re-layouts  39.2 us (19%)
  waiting for transfers between devices  32.2 us (16%)
  matrix products  19.7 us (10%)
  other arithmetic  14.9 us (7%)
  between operations  10.2 us (5%)
  starting transfers between devices  5.37 us (3%)
    all_to_all x1, blocking collectives, local(): lax.all_to_all(planes, 'pen', split_axis=2, concat_axis=1, tiled=True)  60.7 us
    all_to_all x1, waiting for transfers between devices, local(): lax.all_to_all(magnet, 'pen', split_axis=1, concat_axis=2, tiled=True)  32.2 us
    all_gather x2, blocking collectives, plane_ghosts(): blocks = lax.all_gather(layers[None], 'blk', axis=0, tiled=True)  21.8 us
    dot_general x2, matrix products, local(): jnp.einsum('fcy,fzyx->fzcx', inv_y, swept_x, preferred_element_type=jnp.f...  19.7 us
    another operation x2, other arithmetic  11.9 us
    gather x8, local copies, waits for them, and re-layouts, plane_ghosts(): result.append(jnp.take(segment, take_at, axis=-1))  11.6 us
    unnamed x27, local copies, waits for them, and re-layouts  9.01 us
    another operation x1, local copies, waits for them, and re-layouts, local(): planes = jnp.stack([new_proton, new_carbon]).astype(jnp.bfloat16)  7.86 us
  transfers between devices with their start and end apart: 1, of which 1 were waited for; matrix products, arithmetic and copies ran while one was open for 2% of the time, Pallas kernels for 0%

commit v1 on v0

v1 whole, which is shorter than its diff:
```python
import functools
import jax
import jax.numpy as jnp
from jax import lax
from jax.experimental import pallas as pl
from jax.experimental.pallas import tpu as pltpu
from jax.sharding import PartitionSpec as P

STEPS = 2
LANES = 128
NT = (((1,), (1,)), ((), ()))


def dot(a, b):
    return jnp.dot(a, b, preferred_element_type=jnp.float32)


def dot_nt(a, b):
    return lax.dot_general(a, b, NT, preferred_element_type=jnp.float32)


def kernel(n_pen, n_blk, rates, partner, side, orient, offset, state, inv_x, inv_y, out,
           planes, swept, op_x, op_xt, op_y, perm, layers,
           in_send, in_recv, out_send, out_recv, g_send, g_recv, own_sem, op_sem):
    blk = lax.axis_index("blk")
    pen = lax.axis_index("pen")
    rows = state.shape[3]
    z_per = planes.shape[1]
    gy, gx = planes.shape[2], planes.shape[3]

    barrier = pltpu.get_barrier_semaphore()
    for d in range(1, n_pen):
        pl.semaphore_signal(barrier, inc=1, device_id=(blk, lax.rem(pen + d, n_pen)),
                            device_id_type=pl.DeviceIdType.MESH)
    for d in range(1, n_blk):
        pl.semaphore_signal(barrier, inc=1, device_id=(lax.rem(blk + d, n_blk), pen),
                            device_id_type=pl.DeviceIdType.MESH)
    pl.semaphore_wait(barrier, n_pen + n_blk - 2)

    def in_copy(z, d):
        to = lax.rem(pen + d, n_pen)
        return pltpu.make_async_remote_copy(
            src_ref=state.at[0, :, to * z_per + z],
            dst_ref=planes.at[:, z, pl.ds(pen * rows, rows)],
            send_sem=in_send.at[z, d], recv_sem=in_recv.at[z, d],
            device_id=(blk, to), device_id_type=pl.DeviceIdType.MESH)

    def in_arrival(z, d):
        came = lax.rem(pen + n_pen - d, n_pen)
        return pltpu.make_async_remote_copy(
            src_ref=state.at[0, :, came * z_per + z],
            dst_ref=planes.at[:, z, pl.ds(came * rows, rows)],
            send_sem=in_send.at[z, d], recv_sem=in_recv.at[z, d],
            device_id=(blk, came), device_id_type=pl.DeviceIdType.MESH)

    def in_own(z):
        return pltpu.make_async_copy(
            state.at[0, :, pen * z_per + z], planes.at[:, z, pl.ds(pen * rows, rows)], own_sem.at[0, z])

    def out_copy(z, d):
        to = lax.rem(pen + d, n_pen)
        return pltpu.make_async_remote_copy(
            src_ref=planes.at[:, z, pl.ds(to * rows, rows)],
            dst_ref=out.at[0, :, pen * z_per + z],
            send_sem=out_send.at[z, d], recv_sem=out_recv.at[z, d],
            device_id=(blk, to), device_id_type=pl.DeviceIdType.MESH)

    def out_arrival(z, d):
        came = lax.rem(pen + n_pen - d, n_pen)
        return pltpu.make_async_remote_copy(
            src_ref=planes.at[:, z, pl.ds(came * rows, rows)],
            dst_ref=out.at[0, :, came * z_per + z],
            send_sem=out_send.at[z, d], recv_sem=out_recv.at[z, d],
            device_id=(blk, came), device_id_type=pl.DeviceIdType.MESH)

    def out_own(z):
        return pltpu.make_async_copy(
            planes.at[:, z, pl.ds(pen * rows, rows)], out.at[0, :, pen * z_per + z], own_sem.at[1, z])

    def ghost_copy(slot, d):
        return pltpu.make_async_remote_copy(
            src_ref=layers.at[slot, blk], dst_ref=layers.at[slot, blk],
            send_sem=g_send.at[slot, d], recv_sem=g_recv.at[slot, d],
            device_id=(lax.rem(blk + d, n_blk), pen), device_id_type=pl.DeviceIdType.MESH)

    def ghost_arrival(slot, d):
        came = lax.rem(blk + n_blk - d, n_blk)
        return pltpu.make_async_remote_copy(
            src_ref=layers.at[slot, came], dst_ref=layers.at[slot, came],
            send_sem=g_send.at[slot, d], recv_sem=g_recv.at[slot, d],
            device_id=(came, pen), device_id_type=pl.DeviceIdType.MESH)

    @pl.loop(0, z_per)
    def _(z):
        for d in range(1, n_pen):
            in_copy(z, d).start()
        in_own(z).start()

    load_x = pltpu.make_async_copy(inv_x.at[0], op_x, op_sem.at[0])
    load_y = pltpu.make_async_copy(inv_y.at[0], op_y, op_sem.at[1])
    load_x.start()
    load_y.start()

    at_j = lax.broadcasted_iota(jnp.int32, (gy, gy), 0)
    at_y = lax.broadcasted_iota(jnp.int32, (gy, gy), 1)
    for k in range(2):
        take = jnp.where(orient[0, k] == 1, gy - 1 - at_j, at_j) + offset[0, k] * rows
        take = jnp.where(take >= gy, take - gy, take)
        perm[k] = jnp.where(take == at_y, 1.0, 0.0).astype(jnp.bfloat16)
    eye = jnp.where(at_j == at_y, 1.0, 0.0).astype(jnp.bfloat16)
    load_x.wait()
    for f in range(2):
        op_xt[f] = dot_nt(eye, op_x[f]).astype(jnp.bfloat16)
    load_y.wait()

    pick_row = lax.broadcasted_iota(jnp.int32, (16, LANES), 0)
    pick_lane = lax.broadcasted_iota(jnp.int32, (16, LANES), 1)
    lane = lax.broadcasted_iota(jnp.int32, (gy, LANES), 1)
    ends = ((0, 0), (gx - LANES, LANES - 1))
    half = gx // 2

    @pl.loop(0, z_per)
    def _(z):
        for d in range(1, n_pen):
            in_arrival(z, d).wait_recv()
        in_own(z).wait()

        @pl.loop(0, STEPS)
        def _(step):
            slot = z * STEPS + step
            mine = jnp.zeros((16, gy), jnp.float32)
            for k, (first, at) in enumerate(ends):
                for f in range(2):
                    pick = jnp.where((pick_row == 2 * k + f) & (pick_lane == at), 1.0, 0.0).astype(jnp.bfloat16)
                    mine += dot_nt(pick, planes[f, z, :, first:first + LANES])
            layers[slot, blk] = mine.astype(jnp.bfloat16)
            for d in range(1, n_blk):
                ghost_copy(slot, d).start()
            for d in range(1, n_blk):
                ghost_arrival(slot, d).wait_recv()

            for k, (first, at) in enumerate(ends):
                layer = layers[slot, 0]
                for b in range(1, n_blk):
                    layer = jnp.where(partner[0, k] == b, layers[slot, b], layer)
                ghosts = dot_nt(perm[k], layer)
                for f in range(2):
                    ghost = jnp.where(side[0, k] == 1, ghosts[:, 2 + f:3 + f], ghosts[:, f:f + 1])
                    cells = planes[f, z, :, first:first + LANES].astype(jnp.float32)
                    planes[f, z, :, first:first + LANES] = (
                        cells + jnp.where(lane == at, ghost, 0.0)).astype(jnp.bfloat16)

            for f in range(2):
                for n in range(2):
                    swept[f, :, n * half:(n + 1) * half] = dot(
                        planes[f, z], op_xt[f, :, n * half:(n + 1) * half]).astype(jnp.bfloat16)
            for n in range(2):
                proton = dot(op_y[0], swept[0, :, n * half:(n + 1) * half])
                carbon = dot(op_y[1], swept[1, :, n * half:(n + 1) * half])
                new_proton = proton - (rates[0, 0] * proton + rates[0, 2] * carbon)
                new_carbon = carbon - (rates[0, 1] * carbon + rates[0, 2] * proton)
                planes[0, z, :, n * half:(n + 1) * half] = new_proton.astype(jnp.bfloat16)
                planes[1, z, :, n * half:(n + 1) * half] = new_carbon.astype(jnp.bfloat16)

        for d in range(1, n_pen):
            out_copy(z, d).start()
        out_own(z).start()

    @pl.loop(0, z_per)
    def _(z):
        for d in range(1, n_pen):
            in_copy(z, d).wait_send()
            out_copy(z, d).wait_send()
            out_arrival(z, d).wait_recv()
        out_own(z).wait()
        for step in range(STEPS):
            for d in range(1, n_blk):
                ghost_copy(z * STEPS + step, d).wait_send()


def solution(mesh):
    n_pen, n_blk = mesh.shape["pen"], mesh.shape["blk"]

    def local(state, inverse_x, inverse_y, rates, partner, face_side, orient, offset):
        _, fields, gz, rows, gx = state.shape
        z_per, gy = gz // n_pen, rows * n_pen
        slots = z_per * STEPS
        smem = pl.BlockSpec(memory_space=pltpu.SMEM)
        anywhere = pl.BlockSpec(memory_space=pl.ANY)
        bf16 = jnp.bfloat16
        return pl.pallas_call(
            functools.partial(kernel, n_pen, n_blk),
            out_shape=jax.ShapeDtypeStruct(state.shape, state.dtype),
            in_specs=[smem] * 5 + [anywhere] * 3,
            out_specs=anywhere,
            scratch_shapes=[
                pltpu.VMEM((fields, z_per, gy, gx), bf16),
                pltpu.VMEM((fields, gy, gx), bf16),
                pltpu.VMEM((fields, gx, gx), bf16),
                pltpu.VMEM((fields, gx, gx), bf16),
                pltpu.VMEM((fields, gy, gy), bf16),
                pltpu.VMEM((2, gy, gy), bf16),
                pltpu.VMEM((slots, n_blk, 16, gy), bf16),
                pltpu.SemaphoreType.DMA((z_per, n_pen)),
                pltpu.SemaphoreType.DMA((z_per, n_pen)),
                pltpu.SemaphoreType.DMA((z_per, n_pen)),
                pltpu.SemaphoreType.DMA((z_per, n_pen)),
                pltpu.SemaphoreType.DMA((slots, n_blk)),
                pltpu.SemaphoreType.DMA((slots, n_blk)),
                pltpu.SemaphoreType.DMA((2, z_per)),
                pltpu.SemaphoreType.DMA((2,)),
            ],
            compiler_params=pltpu.CompilerParams(
                collective_id=0, has_side_effects=True, vmem_limit_bytes=60 * 1024 * 1024),
            cost_estimate=pl.CostEstimate(
                flops=8 * STEPS * z_per * gy * gx * (gx + gy) // 2,
                bytes_accessed=4 * state.size + 8 * gx * gx, transcendentals=0),
        )(rates, partner, face_side, orient, offset, state, inverse_x, inverse_y)

    line = P("blk", None)
    return jax.shard_map(
        local,
        mesh=mesh,
        in_specs=(
            P("blk", None, None, "pen", None),
            P("blk", None, None, None),
            P("blk", None, None, None),
            line, line, line, line, line,
        ),
        out_specs=P("blk", None, None, "pen", None),
        check_vma=False,
    )
```

time: 206 us -> 104 us (0.50); the launches traced: 204 us -> 104 us
  Pallas kernels: 0 us -> 99.4 us
  blocking collectives: 82.5 us -> 0 us
  local copies, waits for them, and re-layouts: 39.2 us -> 4.7 us
  waiting for transfers between devices: 32.2 us -> 0 us
  matrix products: 19.7 us -> 0 us
  other arithmetic: 14.9 us -> 0 us
  between operations: 10.2 us -> 0.01 us
  starting transfers between devices: 5.37 us -> 0 us
    pallas_call x0 -> x1, Pallas kernels: none -> 99.4 us  [local(): pl.pallas_call(functools.partial(kernel, n_pen, n_blk), out_shape=jax.Sha...]
    all_to_all x1 -> x0, blocking collectives: 60.7 us -> none  [local(): lax.all_to_all(planes, 'pen', split_axis=2, concat_axis=1, tiled=True)]
    all_to_all x1 -> x0, waiting for transfers between devices: 32.2 us -> none  [local(): lax.all_to_all(magnet, 'pen', split_axis=1, concat_axis=2, tiled=True)]
    all_gather x2 -> x0, blocking collectives: 21.8 us -> none  [plane_ghosts(): blocks = lax.all_gather(layers[None], 'blk', axis=0, tiled=True)]
    dot_general x2 -> x0, matrix products: 19.7 us -> none  [local(): jnp.einsum('fcy,fzyx->fzcx', inv_y, swept_x, preferred_element_type=jnp.f...]
    another operation x5 -> x0, other arithmetic: 14.4 us -> none
    gather x8 -> x0, local copies, waits for them, and re-layouts: 11.6 us -> none  [plane_ghosts(): result.append(jnp.take(segment, take_at, axis=-1))]
    another operation x1 -> x0, local copies, waits for them, and re-layouts: 7.86 us -> none  [local(): planes = jnp.stack([new_proton, new_carbon]).astype(jnp.bfloat16)]
  transfers between devices with their start and end apart: 1 -> 0, of which waited for: 1 -> 0; matrix products, arithmetic and copies ran while one was open for 2% -> 0% of each run, Pallas kernels for 0% -> 0%
where the time goes in v1:
time: 104 us
  Pallas kernels  99.4 us (96%)
  local copies, waits for them, and re-layouts  4.7 us (5%)
    pallas_call x1, Pallas kernels, local(): pl.pallas_call(functools.partial(kernel, n_pen, n_blk), out_shape=jax.Sha...  99.4 us
    unnamed x1, local copies, waits for them, and re-layouts  4.7 us

profile of v1, /device:TPU:1, one launch (start us, length us, event | category | flops | bytes accessed | tf_op | source)
XLA Modules:
  0.0 104.1 jit_solution(13945910213848504030)
XLA Ops:
  0.0 99.4 %shard_map.82 = bf16[1,2,32,64,512]{4,3,2,1,0:T(8,128)(2,1)} custom-call(f32[1,3]{1,0:T(1,128)} %rates.1, s32[1,2]{1,0:T(1,128)} %partner.1, s32[1,2]{1,0:T(1,128)} %side.1, s32[1,2]{1,0:T(1,128)} %orient.1, s32[1,2]{1,0:T(1,128)} %offset.1, bf16[1,2,32,64,512]{4,3,2,1,0:T(8,128)(2,1)} %state.1, bf16[1,2,512,512]{3,2,1,0:T(8,128)(2,1)} %inv_x.1, ...), custom_call_target="tpu_custom_call" | custom-call | flops 8589934592 | bytes 10485760 | tf_op jit(solution)/shard_map/pallas_call | solution.py:191
  99.4 4.7 %copy.10 = bf16[1,2,32,64,512]{4,3,2,1,0:T(8,128)(2,1)} copy(bf16[1,2,32,64,512]{4,3,2,1,0:T(8,128)(2,1)} %shard_map.82) | data formatting | bytes 8388608

commit v2 on v1

--- a/solution.py
+++ b/solution.py
@@ -17,6 +17,18 @@
 
 def dot_nt(a, b):
     return lax.dot_general(a, b, NT, preferred_element_type=jnp.float32)
+
+
+def partner_of(pen, d, n_pen):
+    if n_pen & (n_pen - 1) or n_pen < 8:
+        return lax.rem(pen + d, n_pen)
+    core = lax.rem(pen, 2)
+    swapped = (d & ~6) | (d & 2) << 1 | (d & 4) >> 1
+    other = pen
+    for bit in (1 << b for b in range(n_pen.bit_length() - 1)):
+        flip = (1 - core) * int(d & bit > 0) + core * int(swapped & bit > 0)
+        other = other + flip * bit * (1 - 2 * lax.rem(pen // bit, 2))
+    return other
 
 
 def kernel(n_pen, n_blk, rates, partner, side, orient, offset, state, inv_x, inv_y, out,
@@ -28,49 +40,48 @@
     z_per = planes.shape[1]
     gy, gx = planes.shape[2], planes.shape[3]
 
+    order = (2, 4, 6, 3, 5, 7, 1) if n_pen == 8 else range(1, n_pen)
+    partners = [partner_of(pen, d, n_pen) for d in order]
+
     barrier = pltpu.get_barrier_semaphore()
-    for d in range(1, n_pen):
-        pl.semaphore_signal(barrier, inc=1, device_id=(blk, lax.rem(pen + d, n_pen)),
+    for to in partners:
+        pl.semaphore_signal(barrier, inc=1, device_id=(blk, to),
                             device_id_type=pl.DeviceIdType.MESH)
     for d in range(1, n_blk):
         pl.semaphore_signal(barrier, inc=1, device_id=(lax.rem(blk + d, n_blk), pen),
                             device_id_type=pl.DeviceIdType.MESH)
     pl.semaphore_wait(barrier, n_pen + n_blk - 2)
 
-    def in_copy(z, d):
-        to = lax.rem(pen + d, n_pen)
+    def in_copy(z, to):
         return pltpu.make_async_remote_copy(
             src_ref=state.at[0, :, to * z_per + z],
             dst_ref=planes.at[:, z, pl.ds(pen * rows, rows)],
-            send_sem=in_send.at[z, d], recv_sem=in_recv.at[z, d],
+            send_sem=in_send.at[z, to], recv_sem=in_recv.at[z, pen],
             device_id=(blk, to), device_id_type=pl.DeviceIdType.MESH)
 
-    def in_arrival(z, d):
-        came = lax.rem(pen + n_pen - d, n_pen)
+    def in_arrival(z, came):
         return pltpu.make_async_remote_copy(
             src_ref=state.at[0, :, came * z_per + z],
             dst_ref=planes.at[:, z, pl.ds(came * rows, rows)],
-            send_sem=in_send.at[z, d], recv_sem=in_recv.at[z, d],
+            send_sem=in_send.at[z, came], recv_sem=in_recv.at[z, came],
             device_id=(blk, came), device_id_type=pl.DeviceIdType.MESH)
 
     def in_own(z):
         return pltpu.make_async_copy(
             state.at[0, :, pen * z_per + z], planes.at[:, z, pl.ds(pen * rows, rows)], own_sem.at[0, z])
 
-    def out_copy(z, d):
-        to = lax.rem(pen + d, n_pen)
+    def out_copy(z, to):
         return pltpu.make_async_remote_copy(
             src_ref=planes.at[:, z, pl.ds(to * rows, rows)],
             dst_ref=out.at[0, :, pen * z_per + z],
-            send_sem=out_send.at[z, d], recv_sem=out_recv.at[z, d],
+            send_sem=out_send.at[z, to], recv_sem=out_recv.at[z, pen],
             device_id=(blk, to), device_id_type=pl.DeviceIdType.MESH)
 
-    def out_arrival(z, d):
-        came = lax.rem(pen + n_pen - d, n_pen)
+    def out_arrival(z, came):
         return pltpu.make_async_remote_copy(
             src_ref=planes.at[:, z, pl.ds(came * rows, rows)],
             dst_ref=out.at[0, :, came * z_per + z],
-            send_sem=out_send.at[z, d], recv_sem=out_recv.at[z, d],
+            send_sem=out_send.at[z, came], recv_sem=out_recv.at[z, came],
             device_id=(blk, came), device_id_type=pl.DeviceIdType.MESH)
 
     def out_own(z):
@@ -90,11 +101,13 @@
             send_sem=g_send.at[slot, d], recv_sem=g_recv.at[slot, d],
             device_id=(came, pen), device_id_type=pl.DeviceIdType.MESH)
 
-    @pl.loop(0, z_per)
-    def _(z):
-        for d in range(1, n_pen):
-            in_copy(z, d).start()
+    def send_in(z):
+        for to in partners:
+            in_copy(z, to).start()
         in_own(z).start()
+
+    ahead = min(2, z_per)
+    pl.loop(0, ahead)(send_in)
 
     load_x = pltpu.make_async_copy(inv_x.at[0], op_x, op_sem.at[0])
     load_y = pltpu.make_async_copy(inv_y.at[0], op_y, op_sem.at[1])
@@ -121,9 +134,10 @@
 
     @pl.loop(0, z_per)
     def _(z):
-        for d in range(1, n_pen):
-            in_arrival(z, d).wait_recv()
+        for came in partners:
+            in_arrival(z, came).wait_recv()
         in_own(z).wait()
+        pl.when(z + ahead < z_per)(lambda: send_in(z + ahead))
 
         @pl.loop(0, STEPS)
         def _(step):
@@ -162,16 +176,16 @@
                 planes[0, z, :, n * half:(n + 1) * half] = new_proton.astype(jnp.bfloat16)
                 planes[1, z, :, n * half:(n + 1) * half] = new_carbon.astype(jnp.bfloat16)
 
-        for d in range(1, n_pen):
-            out_copy(z, d).start()
+        for to in partners:
+            out_copy(z, to).start()
         out_own(z).start()
 
     @pl.loop(0, z_per)
     def _(z):
-        for d in range(1, n_pen):
-            in_copy(z, d).wait_send()
-            out_copy(z, d).wait_send()
-            out_arrival(z, d).wait_recv()
+        for to in partners:
+            in_copy(z, to).wait_send()
+            out_copy(z, to).wait_send()
+            out_arrival(z, to).wait_recv()
         out_own(z).wait()
         for step in range(STEPS):
             for d in range(1, n_blk):
@@ -185,12 +199,13 @@
         _, fields, gz, rows, gx = state.shape
         z_per, gy = gz // n_pen, rows * n_pen
         slots = z_per * STEPS
+        keep = functools.partial(pltpu.with_memory_space_constraint, memory_space=pltpu.HBM)
         smem = pl.BlockSpec(memory_space=pltpu.SMEM)
         anywhere = pl.BlockSpec(memory_space=pl.ANY)
         bf16 = jnp.bfloat16
         return pl.pallas_call(
             functools.partial(kernel, n_pen, n_blk),
-            out_shape=jax.ShapeDtypeStruct(state.shape, state.dtype),
+            out_shape=pltpu.VMEM(state.shape, state.dtype),
             in_specs=[smem] * 5 + [anywhere] * 3,
             out_specs=anywhere,
             scratch_shapes=[
@@ -211,11 +226,11 @@
                 pltpu.SemaphoreType.DMA((2,)),
             ],
             compiler_params=pltpu.CompilerParams(
-                collective_id=0, has_side_effects=True, vmem_limit_bytes=60 * 1024 * 1024),
+                collective_id=0, has_side_effects=True, vmem_limit_bytes=48 * 1024 * 1024),
             cost_estimate=pl.CostEstimate(
                 flops=8 * STEPS * z_per * gy * gx * (gx + gy) // 2,
                 bytes_accessed=4 * state.size + 8 * gx * gx, transcendentals=0),
-        )(rates, partner, face_side, orient, offset, state, inverse_x, inverse_y)
+        )(*map(keep, (rates, partner, face_side, orient, offset, state, inverse_x, inverse_y)))
 
     line = P("blk", None)
     return jax.shard_map(

time: 104 us -> 102 us (0.981)
  local copies, waits for them, and re-layouts: 4.7 us -> 2.02 us
    unnamed x1, local copies, waits for them, and re-layouts: 4.7 us -> 2.02 us
where the time goes in v2:
time: 102 us
  Pallas kernels  99.9 us (98%)
  local copies, waits for them, and re-layouts  2.02 us (2%)
    pallas_call x1, Pallas kernels, local(): pl.pallas_call(functools.partial(kernel, n_pen, n_blk), out_shape=pltpu.V...  99.9 us

profile of v2, /device:TPU:1, one launch (start us, length us, event | category | flops | bytes accessed | tf_op | source)
XLA Modules:
  0.0 102.0 jit_solution(12720439873628684729)
XLA Ops:
  0.0 99.9 %shard_map.82 = bf16[1,2,32,64,512]{4,3,2,1,0:T(8,128)(2,1)S(1)} custom-call(f32[1,3]{1,0:T(1,128)} %rates.1, s32[1,2]{1,0:T(1,128)} %partner.1, s32[1,2]{1,0:T(1,128)} %side.1, s32[1,2]{1,0:T(1,128)} %orient.1, s32[1,2]{1,0:T(1,128)} %offset.1, bf16[1,2,32,64,512]{4,3,2,1,0:T(8,128)(2,1)} %state.1, bf16[1,2,512,512]{3,2,1,0:T(8,128)(2,1)} %inv_x.1, ...), custom_call_target="tpu_custom_call" | custom-call | flops 8589934592 | bytes 10485760 | tf_op jit(solution)/shard_map/pallas_call | solution.py:206
  100.0 2.0 %copy.10 = bf16[1,2,32,64,512]{4,3,2,1,0:T(8,128)(2,1)} copy(bf16[1,2,32,64,512]{4,3,2,1,0:T(8,128)(2,1)S(1)} %shard_map.82) | data formatting | bytes 8388608

commit v3 on v2

--- a/solution.py
+++ b/solution.py
@@ -132,53 +132,63 @@
     ends = ((0, 0), (gx - LANES, LANES - 1))
     half = gx // 2
 
-    @pl.loop(0, z_per)
+    def send_layers(z, slot):
+        mine = jnp.zeros((16, gy), jnp.float32)
+        for k, (first, at) in enumerate(ends):
+            for f in range(2):
+                pick = jnp.where((pick_row == 2 * k + f) & (pick_lane == at), 1.0, 0.0).astype(jnp.bfloat16)
+                mine += dot_nt(pick, planes[f, z, :, first:first + LANES])
+        layers[slot, blk] = mine.astype(jnp.bfloat16)
+        for d in range(1, n_blk):
+            ghost_copy(slot, d).start()
+
+    def sweep(z, slot):
+        for d in range(1, n_blk):
+            ghost_arrival(slot, d).wait_recv()
+        for k, (first, at) in enumerate(ends):
+            layer = layers[slot, 0]
+            for b in range(1, n_blk):
+                layer = jnp.where(partner[0, k] == b, layers[slot, b], layer)
+            ghosts = dot_nt(perm[k], layer)
+            for f in range(2):
+                ghost = jnp.where(side[0, k] == 1, ghosts[:, 2 + f:3 + f], ghosts[:, f:f + 1])
+                cells = planes[f, z, :, first:first + LANES].astype(jnp.float32)
+                planes[f, z, :, first:first + LANES] = (
+                    cells + jnp.where(lane == at, ghost, 0.0)).astype(jnp.bfloat16)
+
+        for f in range(2):
+            for n in range(2):
+                swept[f, :, n * half:(n + 1) * half] = dot(
+                    planes[f, z], op_xt[f, :, n * half:(n + 1) * half]).astype(jnp.bfloat16)
+        for n in range(2):
+            proton = dot(op_y[0], swept[0, :, n * half:(n + 1) * half])
+            carbon = dot(op_y[1], swept[1, :, n * half:(n + 1) * half])
+            new_proton = proton - (rates[0, 0] * proton + rates[0, 2] * carbon)
+            new_carbon = carbon - (rates[0, 1] * carbon + rates[0, 2] * proton)
+            planes[0, z, :, n * half:(n + 1) * half] = new_proton.astype(jnp.bfloat16)
+            planes[1, z, :, n * half:(n + 1) * half] = new_carbon.astype(jnp.bfloat16)
+
+    @pl.loop(0, z_per + 1)
     def _(z):
-        for came in partners:
-            in_arrival(z, came).wait_recv()
-        in_own(z).wait()
-        pl.when(z + ahead < z_per)(lambda: send_in(z + ahead))
-
-        @pl.loop(0, STEPS)
-        def _(step):
-            slot = z * STEPS + step
-            mine = jnp.zeros((16, gy), jnp.float32)
-            for k, (first, at) in enumerate(ends):
-                for f in range(2):
-                    pick = jnp.where((pick_row == 2 * k + f) & (pick_lane == at), 1.0, 0.0).astype(jnp.bfloat16)
-                    mine += dot_nt(pick, planes[f, z, :, first:first + LANES])
-            layers[slot, blk] = mine.astype(jnp.bfloat16)
-            for d in range(1, n_blk):
-                ghost_copy(slot, d).start()
-            for d in range(1, n_blk):
-                ghost_arrival(slot, d).wait_recv()
-
-            for k, (first, at) in enumerate(ends):
-                layer = layers[slot, 0]
-                for b in range(1, n_blk):
-                    layer = jnp.where(partner[0, k] == b, layers[slot, b], layer)
-                ghosts = dot_nt(perm[k], layer)
-                for f in range(2):
-                    ghost = jnp.where(side[0, k] == 1, ghosts[:, 2 + f:3 + f], ghosts[:, f:f + 1])
-                    cells = planes[f, z, :, first:first + LANES].astype(jnp.float32)
-                    planes[f, z, :, first:first + LANES] = (
-                        cells + jnp.where(lane == at, ghost, 0.0)).astype(jnp.bfloat16)
-
-            for f in range(2):
-                for n in range(2):
-                    swept[f, :, n * half:(n + 1) * half] = dot(
-                        planes[f, z], op_xt[f, :, n * half:(n + 1) * half]).astype(jnp.bfloat16)
-            for n in range(2):
-                proton = dot(op_y[0], swept[0, :, n * half:(n + 1) * half])
-                carbon = dot(op_y[1], swept[1, :, n * half:(n + 1) * half])
-                new_proton = proton - (rates[0, 0] * proton + rates[0, 2] * carbon)
-                new_carbon = carbon - (rates[0, 1] * carbon + rates[0, 2] * proton)
-                planes[0, z, :, n * half:(n + 1) * half] = new_proton.astype(jnp.bfloat16)
-                planes[1, z, :, n * half:(n + 1) * half] = new_carbon.astype(jnp.bfloat16)
-
-        for to in partners:
-            out_copy(z, to).start()
-        out_own(z).start()
+        @pl.when(z < z_per)
+        def _():
+            for came in partners:
+                in_arrival(z, came).wait_recv()
+            in_own(z).wait()
+            pl.when(z + ahead < z_per)(lambda: send_in(z + ahead))
+            send_layers(z, STEPS * z)
+
+        @pl.when(z > 0)
+        def _():
+            sweep(z - 1, STEPS * z - 1)
+            for to in partners:
+                out_copy(z - 1, to).start()
+            out_own(z - 1).start()
+
+        @pl.when(z < z_per)
+        def _():
+            sweep(z, STEPS * z)
+            send_layers(z, STEPS * z + 1)
 
     @pl.loop(0, z_per)
     def _(z):

time: 102 us -> 102 us (level)
  no operation moved by 1% of the time
where the time goes in v3:
time: 102 us
  Pallas kernels  99.9 us (98%)
  local copies, waits for them, and re-layouts  2.02 us (2%)
    pallas_call x1, Pallas kernels, local(): pl.pallas_call(functools.partial(kernel, n_pen, n_blk), out_shape=pltpu.V...  99.9 us

profile of v3, /device:TPU:1, one launch (start us, length us, event | category | flops | bytes accessed | tf_op | source)
XLA Modules:
  0.0 102.0 jit_solution(7186827615155032417)
XLA Ops:
  0.0 99.9 %shard_map.82 = bf16[1,2,32,64,512]{4,3,2,1,0:T(8,128)(2,1)S(1)} custom-call(f32[1,3]{1,0:T(1,128)} %rates.1, s32[1,2]{1,0:T(1,128)} %partner.1, s32[1,2]{1,0:T(1,128)} %side.1, s32[1,2]{1,0:T(1,128)} %orient.1, s32[1,2]{1,0:T(1,128)} %offset.1, bf16[1,2,32,64,512]{4,3,2,1,0:T(8,128)(2,1)} %state.1, bf16[1,2,512,512]{3,2,1,0:T(8,128)(2,1)} %inv_x.1, ...), custom_call_target="tpu_custom_call" | custom-call | flops 8589934592 | bytes 10485760 | tf_op jit(solution)/shard_map/pallas_call | solution.py:216
  100.0 2.0 %copy.10 = bf16[1,2,32,64,512]{4,3,2,1,0:T(8,128)(2,1)} copy(bf16[1,2,32,64,512]{4,3,2,1,0:T(8,128)(2,1)S(1)} %shard_map.82) | data formatting | bytes 8388608

commit v4 on v3

--- a/solution.py
+++ b/solution.py
@@ -106,8 +106,7 @@
             in_copy(z, to).start()
         in_own(z).start()
 
-    ahead = min(2, z_per)
-    pl.loop(0, ahead)(send_in)
+    pl.loop(0, z_per)(send_in)
 
     load_x = pltpu.make_async_copy(inv_x.at[0], op_x, op_sem.at[0])
     load_y = pltpu.make_async_copy(inv_y.at[0], op_y, op_sem.at[1])
@@ -175,7 +174,6 @@
             for came in partners:
                 in_arrival(z, came).wait_recv()
             in_own(z).wait()
-            pl.when(z + ahead < z_per)(lambda: send_in(z + ahead))
             send_layers(z, STEPS * z)
 
         @pl.when(z > 0)

time: 102 us -> 102 us (level)
  no operation moved by 1% of the time
where the time goes in v4:
time: 102 us
  Pallas kernels  99.9 us (98%)
  local copies, waits for them, and re-layouts  2.02 us (2%)
    pallas_call x1, Pallas kernels, local(): pl.pallas_call(functools.partial(kernel, n_pen, n_blk), out_shape=pltpu.V...  99.9 us

profile of v4, /device:TPU:1, one launch (start us, length us, event | category | flops | bytes accessed | tf_op | source)
XLA Modules:
  0.0 102.0 jit_solution(13116464678127678264)
XLA Ops:
  0.0 99.9 %shard_map.82 = bf16[1,2,32,64,512]{4,3,2,1,0:T(8,128)(2,1)S(1)} custom-call(f32[1,3]{1,0:T(1,128)} %rates.1, s32[1,2]{1,0:T(1,128)} %partner.1, s32[1,2]{1,0:T(1,128)} %side.1, s32[1,2]{1,0:T(1,128)} %orient.1, s32[1,2]{1,0:T(1,128)} %offset.1, bf16[1,2,32,64,512]{4,3,2,1,0:T(8,128)(2,1)} %state.1, bf16[1,2,512,512]{3,2,1,0:T(8,128)(2,1)} %inv_x.1, ...), custom_call_target="tpu_custom_call" | custom-call | flops 8589934592 | bytes 10485760 | tf_op jit(solution)/shard_map/pallas_call | solution.py:214
  100.0 2.0 %copy.10 = bf16[1,2,32,64,512]{4,3,2,1,0:T(8,128)(2,1)} copy(bf16[1,2,32,64,512]{4,3,2,1,0:T(8,128)(2,1)S(1)} %shard_map.82) | data formatting | bytes 8388608

commit v5 on v4

--- a/solution.py
+++ b/solution.py
@@ -17,18 +17,6 @@
 
 def dot_nt(a, b):
     return lax.dot_general(a, b, NT, preferred_element_type=jnp.float32)
-
-
-def partner_of(pen, d, n_pen):
-    if n_pen & (n_pen - 1) or n_pen < 8:
-        return lax.rem(pen + d, n_pen)
-    core = lax.rem(pen, 2)
-    swapped = (d & ~6) | (d & 2) << 1 | (d & 4) >> 1
-    other = pen
-    for bit in (1 << b for b in range(n_pen.bit_length() - 1)):
-        flip = (1 - core) * int(d & bit > 0) + core * int(swapped & bit > 0)
-        other = other + flip * bit * (1 - 2 * lax.rem(pen // bit, 2))
-    return other
 
 
 def kernel(n_pen, n_blk, rates, partner, side, orient, offset, state, inv_x, inv_y, out,
@@ -40,8 +28,7 @@
     z_per = planes.shape[1]
     gy, gx = planes.shape[2], planes.shape[3]
 
-    order = (2, 4, 6, 3, 5, 7, 1) if n_pen == 8 else range(1, n_pen)
-    partners = [partner_of(pen, d, n_pen) for d in order]
+    partners = [lax.rem(pen + d, n_pen) for d in range(1, n_pen)]
 
     barrier = pltpu.get_barrier_semaphore()
     for to in partners:

time: 102 us -> 102 us (level)
  no operation moved by 1% of the time
where the time goes in v5:
time: 102 us; the launch traced here: 101 us
  Pallas kernels  99.4 us (97%)
  local copies, waits for them, and re-layouts  2.02 us (2%)
    pallas_call x1, Pallas kernels, local(): pl.pallas_call(functools.partial(kernel, n_pen, n_blk), out_shape=pltpu.V...  99.4 us

profile of v5, /device:TPU:1, one launch (start us, length us, event | category | flops | bytes accessed | tf_op | source)
XLA Modules:
  0.0 101.4 jit_solution(18056367767140048049)
XLA Ops:
  0.0 99.4 %shard_map.82 = bf16[1,2,32,64,512]{4,3,2,1,0:T(8,128)(2,1)S(1)} custom-call(f32[1,3]{1,0:T(1,128)} %rates.1, s32[1,2]{1,0:T(1,128)} %partner.1, s32[1,2]{1,0:T(1,128)} %side.1, s32[1,2]{1,0:T(1,128)} %orient.1, s32[1,2]{1,0:T(1,128)} %offset.1, bf16[1,2,32,64,512]{4,3,2,1,0:T(8,128)(2,1)} %state.1, bf16[1,2,512,512]{3,2,1,0:T(8,128)(2,1)} %inv_x.1, ...), custom_call_target="tpu_custom_call" | custom-call | flops 8589934592 | bytes 10485760 | tf_op jit(solution)/shard_map/pallas_call | solution.py:201
  99.4 2.0 %copy.10 = bf16[1,2,32,64,512]{4,3,2,1,0:T(8,128)(2,1)} copy(bf16[1,2,32,64,512]{4,3,2,1,0:T(8,128)(2,1)S(1)} %shard_map.82) | data formatting | bytes 8388608
